TPU v7x, 32 devices: a whole 2x2x4 slice. The times are simulated.
32 devices in a mesh: tm: 8 (over z, x), sta: 4 (over y, core).
Axes of the slice: x: 2, y: 2, z: 4, core: 2. Of those that a mesh axis runs over, the one named last changes fastest.
Arguments:
- voltages: bfloat16 [2, 4, 64, 262144], P(None, None, 'sta', 'tm'), may hold values from -6 to 6
- sample_delay: int32 [64, 8], P('sta', 'tm'), may hold values from 0 to 8192, as said below
- frac_index: int32 [64, 8], P('sta', 'tm'), may hold values from 0 to 63
- phase_index: int32 [4, 64, 8], P(None, 'sta', 'tm'), may hold values from 0 to 1023
- fringe_rate: float32 [4, 64], P(None, 'sta'), may hold values from -3 to 3
Outputs:
- visibilities: float32 [4, 16384, 64, 128], P(None, ('tm', 'sta'))
Inputs may be any that keep to these rules, and one draw needn't show every extreme that they name: `sample_delay`: the largest delay, 8192, occurs in every draw.
All inputs are finite; a program needn't handle non-finite values.
Results may differ from a plain program's by a relative error of at most 0.0089.
Values may be sent and summed in bfloat16 or wider, within the bound.
A program may use at most 256 MiB of HBM per device.

v0:
```python
import math
import jax
import jax.numpy as jnp
from jax import lax
from jax.sharding import PartitionSpec as P

CHANNELS = 16384
RADIX_A = 128
RADIX_B = 128
TAPS = 32
NFRAC = 64
NPHASE = 1024
MAXD = 8192


def shifted(value, axis, steps):
    count = lax.axis_size(axis)
    first, last = (max(0, -steps), min(count, count - steps))
    return lax.ppermute(value, axis, [(source, source + steps) for source in range(first, last)])


def toeplitz_of(fraction_index):
    inputs_at = jnp.arange(256, dtype=jnp.int32)
    outputs_at = jnp.arange(128, dtype=jnp.int32)
    distance = inputs_at[:, None] - outputs_at[None, :]
    inside = (distance >= 0) & (distance < TAPS)
    fraction = fraction_index.astype(jnp.float32) / NFRAC
    offset = distance.astype(jnp.float32)
    centre = offset[None, :, :] - (TAPS // 2 - 1) - fraction[:, None, None]
    window_taper = 0.5 - 0.5 * jnp.cos(2.0 * jnp.pi * (offset + 0.5) / TAPS)
    values = jnp.sinc(centre) * window_taper[None, :, :]
    return jnp.where(inside[None, :, :], values, 0.0).astype(jnp.bfloat16)


def filter_rows(source, starts, kernel, sample_count):
    slicer = jax.vmap(
        lambda series, start_at: lax.dynamic_slice_in_dim(
            series, start_at, sample_count + 128, axis=1
        ),
        in_axes=(1, 0),
        out_axes=1,
    )
    pieces = slicer(source, starts)
    row_count = pieces.shape[1]
    blocks = sample_count // 128
    tiles = pieces.reshape(2, row_count, blocks + 1, 128)
    upper = jnp.einsum(
        "crnp,rpv->crnv", tiles[:, :, :blocks], kernel[:, :128], preferred_element_type=jnp.float32
    )
    lower = jnp.einsum(
        "crnp,rpv->crnv", tiles[:, :, 1:], kernel[:, 128:], preferred_element_type=jnp.float32
    )
    return (upper + lower).reshape(2, row_count, sample_count)


def rotate_rows(filtered, phase_rows, rate_rows, slice_length):
    sample_count = filtered.shape[-1]
    position = jnp.arange(sample_count, dtype=jnp.int32).astype(jnp.float32) / slice_length
    cycles = (
        phase_rows.astype(jnp.float32)[:, None] / NPHASE + rate_rows[:, None] * position[None, :]
    )
    phase_angle = 2.0 * jnp.pi * cycles
    cosine = jnp.cos(phase_angle)
    sine_value = jnp.sin(phase_angle)
    real_part = filtered[0] * cosine + filtered[1] * sine_value
    imag_part = filtered[1] * cosine - filtered[0] * sine_value
    return jnp.stack([real_part, imag_part]).astype(jnp.bfloat16)


def rotation_table(indices, radix_size):
    product = indices[:, None] * indices[None, :] % radix_size
    table_angle = product.astype(jnp.float32) * (2.0 * math.pi / radix_size)
    scaling = 1.0 / math.sqrt(radix_size)
    cosine = jnp.cos(table_angle) * scaling
    sine_value = jnp.sin(table_angle) * scaling
    stacked = jnp.stack(
        [jnp.stack([cosine, sine_value], axis=1), jnp.stack([-sine_value, cosine], axis=1)], axis=0
    )
    return stacked.astype(jnp.bfloat16)


def dft_tables():
    along_a = jnp.arange(RADIX_A, dtype=jnp.int32)
    along_b = jnp.arange(RADIX_B, dtype=jnp.int32)
    first_table = rotation_table(along_a, RADIX_A)
    second_table = rotation_table(along_b, RADIX_B)
    product = along_a[:, None] * along_b[None, :] % CHANNELS
    twist_angle = product.astype(jnp.float32) * (2.0 * math.pi / CHANNELS)
    twiddle = jnp.stack([jnp.cos(twist_angle), jnp.sin(twist_angle)])
    return (first_table, twiddle, second_table)


def transform(rotated, tables, block_width):
    first_table, twiddle, second_table = tables
    row_count = rotated.shape[1]
    frames = rotated.shape[2] // CHANNELS
    arranged = rotated.reshape(2, row_count, frames, RADIX_A, RADIX_B)
    section_half = jnp.einsum(
        "pkcn,crfnm->prfkm", first_table, arranged, preferred_element_type=jnp.float32
    )
    real_part = section_half[0] * twiddle[0] + section_half[1] * twiddle[1]
    imag_part = section_half[1] * twiddle[0] - section_half[0] * twiddle[1]
    partial_value = jnp.stack([real_part, imag_part]).astype(jnp.bfloat16)
    block_count = CHANNELS // block_width
    if block_width <= RADIX_A:
        split_rows = partial_value.reshape(
            2, row_count, frames, RADIX_A // block_width, block_width, RADIX_B
        )
        spectrum = jnp.einsum(
            "qjpm,prfakm->rfjaqk", second_table, split_rows, preferred_element_type=jnp.float32
        )
    else:
        split_table = second_table.reshape(2, block_count, block_width // RADIX_A, 2, RADIX_B)
        spectrum = jnp.einsum(
            "qJjpm,prfkm->rfJqjk", split_table, partial_value, preferred_element_type=jnp.float32
        )
    return spectrum.astype(jnp.bfloat16).reshape(row_count, frames, block_count, 2 * block_width)


def correlate(spectra):
    frame_total = spectra.shape[2]
    turned = jnp.stack([-spectra[:, :, :, 1], spectra[:, :, :, 0]], axis=3)
    partner = jnp.concatenate([spectra, turned], axis=1)
    summed = jnp.einsum("bifck,bjfck->bkij", spectra, partner, preferred_element_type=jnp.float32)
    return summed / frame_total


def local(voltages, sample_delay, frac_index, phase_index, fringe_rate):
    band_count = voltages.shape[1]
    station_count = voltages.shape[2]
    length = voltages.shape[3]
    frames = length // CHANNELS
    row_count = band_count * station_count
    flattened = voltages.reshape(2, row_count, length)
    delays = jnp.broadcast_to(sample_delay[:, 0][None, :], (band_count, station_count)).reshape(
        row_count
    )
    kernel = toeplitz_of(frac_index[:, 0])
    kernel_rows = jnp.broadcast_to(kernel[None], (band_count,) + kernel.shape).reshape(
        (row_count,) + kernel.shape[1:]
    )
    phase_rows = phase_index[:, :, 0].reshape(row_count)
    rate_rows = fringe_rate.reshape(row_count)
    rim_width = MAXD + TAPS - 1
    following = shifted(flattened[:, :, :rim_width], "tm", -1)
    padding = jnp.zeros((2, row_count, 129 - TAPS), flattened.dtype)
    source = jnp.concatenate([flattened, following, padding], axis=2)
    rotated = rotate_rows(
        filter_rows(source, delays, kernel_rows, length), phase_rows, rate_rows, length
    )
    slices = lax.axis_size("tm")
    groups = lax.axis_size("sta")
    block_width = CHANNELS // (slices * groups)
    spectra = transform(rotated, dft_tables(), block_width)
    packed = spectra.reshape(band_count, station_count, frames, slices, groups, 2 * block_width)
    received = lax.all_to_all(
        lax.all_to_all(packed, "tm", split_axis=3, concat_axis=2, tiled=True),
        "sta",
        split_axis=4,
        concat_axis=1,
        tiled=True,
    )
    gathered = received.reshape(band_count, station_count * groups, slices * frames, 2, block_width)
    return correlate(gathered)


def solution(mesh):
    return jax.shard_map(
        local,
        mesh=mesh,
        in_specs=(
            P(None, None, "sta", "tm"),
            P("sta", "tm"),
            P("sta", "tm"),
            P(None, "sta", "tm"),
            P(None, "sta"),
        ),
        out_specs=P(None, ("tm", "sta"), None, None),
        check_vma=False,
    )
```

profile of v0, /device:TPU:0, one launch (start us, length us, event | category | flops | bytes accessed | tf_op | source)
XLA Modules:
  0.0 952.2 jit_solution(5046426309771215276)
XLA Ops:
  0.0 14.6 %copy.28 = bf16[2,4,16,32768]{3,0,2,1:T(2,128)(2,1)S(1)} copy(bf16[2,4,16,32768]{3,2,1,0:T(8,128)(2,1)} %param.5) | data formatting | bytes 16777216 | tf_op args[0]
  19.4 7.0 constant_dynamic-update-slice_fusion
  32.5 36.5 %collective-permute-done = bf16[2,64,8223]{2,0,1:T(2,128)(2,1)S(1)} collective-permute-done((bf16[2,64,8223]{2,0,1:T(2,128)(2,1)}, bf16[2,64,8223]{2,0,1:T(2,128)(2,1)S(1)}, u32[]{:S(2)}, u32[]{:S(2)}) %collective-permute-start) | collective-permute-done | bytes 2105120 | tf_op jit(solution)/shard_map/ppermute | solution.py:19
  68.9 60.9 %dynamic-update-slice.3 = bf16[2,64,41088]{2,0,1:T(2,128)(2,1)} dynamic-update-slice(bf16[2,64,41088]{2,0,1:T(2,128)(2,1)} %constant_dynamic-update-slice_fusion, bf16[2,64,8223]{2,0,1:T(2,128)(2,1)S(1)} %collective-permute-done, s32[]{} %constant.144, s32[]{} %constant.144, s32[]{} %constant.145) | dynamic-update-slice | bytes 4210180
  129.9 10.2 %dynamic-update-slice.4 = bf16[2,64,41088]{2,0,1:T(2,128)(2,1)} dynamic-update-slice(bf16[2,64,41088]{2,0,1:T(2,128)(2,1)} %dynamic-update-slice.3, bf16[2,64,97]{2,0,1:T(2,128)(2,1)S(1)} %broadcast_in_dim.25, s32[]{} %constant.144, s32[]{} %constant.144, s32[]{} %constant.146) | dynamic-update-slice | bytes 49668 | tf_op jit(solution)/shard_map/concatenate | solution.py:147
  140.0 234.9 %while.1 = (s32[]{:T(128)}, bf16[64,2,41088]{2,1,0:T(2,128)(2,1)}, s32[64,3]{0,1:T(4,128)S(1)}, bf16[64,2,32896]{2,1,0:T(2,128)(2,1)}, s32[]{:T(128)}) while((s32[]{:T(128)}, bf16[64,2,41088]{2,1,0:T(2,128)(2,1)}, s32[64,3]{0,1:T(4,128)S(1)}, bf16[64,2,32896]{2,1,0:T(2,128)(2,1)}, s32[]{:T(128)}) %tuple.32), condition=%wide.while_cond, body=%wide.while_body.sunk | while | flops 2 | bytes 264309 | solution.py:37
  144.4 3.0 dynamic-slice_dynamic-update-slice_fusion.2
  162.7 3.0 dynamic-slice_dynamic-update-slice_fusion.2
  166.4 3.0 dynamic-slice_dynamic-update-slice_fusion.2
  177.4 3.0 dynamic-slice_dynamic-update-slice_fusion.2
  188.4 3.0 dynamic-slice_dynamic-update-slice_fusion.2
  199.4 3.0 dynamic-slice_dynamic-update-slice_fusion.2
  203.1 3.0 dynamic-slice_dynamic-update-slice_fusion.2
  210.5 3.0 dynamic-slice_dynamic-update-slice_fusion.2
  232.5 3.0 dynamic-slice_dynamic-update-slice_fusion.2
  236.1 3.0 dynamic-slice_dynamic-update-slice_fusion.2
  243.5 3.0 dynamic-slice_dynamic-update-slice_fusion.2
  247.1 3.0 dynamic-slice_dynamic-update-slice_fusion.2
  254.5 3.0 dynamic-slice_dynamic-update-slice_fusion.2
  265.5 3.0 dynamic-slice_dynamic-update-slice_fusion.2
  276.5 3.0 dynamic-slice_dynamic-update-slice_fusion.2
  287.5 3.0 dynamic-slice_dynamic-update-slice_fusion.2
  291.2 3.0 dynamic-slice_dynamic-update-slice_fusion.2
  294.9 3.0 dynamic-slice_dynamic-update-slice_fusion.2
  305.9 3.0 dynamic-slice_dynamic-update-slice_fusion.2
  357.2 3.0 dynamic-slice_dynamic-update-slice_fusion.2
  374.9 14.2 %reshape.521 = bf16[2,64,257,128]{3,2,0,1:T(8,128)(2,1)} reshape(bf16[2,64,32896]{2,0,1:T(2,128)(2,1)} %bitcast.99) | data formatting | bytes 16842752 | tf_op jit(solution)/shard_map/reshape | solution.py:46
  391.6 11.9 %fusion.6 = f32[64,128,2,256]{3,1,2,0:T(8,128)} fusion(bf16[2,64,257,128]{3,2,0,1:T(8,128)(2,1)} %reshape.521, bf16[64,256,128]{1,2,0:T(8,128)(2,1)S(1)} %bitcast.97), kind=kOutput, calls=%fused_computation.13 | convolution fusion | flops 1073741824 | bytes 27262976 | tf_op jit(solution)/shard_map/crnp,rpv->crnv/dot_general | solution.py:47
  403.5 16.7 %add_bitcast_fusion = f32[2,64,256,128]{2,3,0,1:T(8,128)} fusion(f32[64,128,2,256]{3,1,2,0:T(8,128)} %fusion.6, bf16[2,64,257,128]{3,2,0,1:T(8,128)(2,1)} %reshape.521, bf16[64,256,128]{1,2,0:T(8,128)(2,1)} %bitcast.98), kind=kOutput, calls=%fused_computation.9 | convolution fusion | flops 1077936128 | bytes 44040192 | tf_op jit(solution)/shard_map/crnp,rpv->crnv/dot_general | solution.py:50
  420.2 11.1 %fusion.78 = (f32[1,64,256,128]{2,3,0,1:T(8,128)}, f32[1,64,256,128]{2,3,0,1:T(8,128)}) fusion(f32[2,64,256,128]{2,3,0,1:T(8,128)} %add_bitcast_fusion), kind=kLoop, calls=%fused_computation.130 | loop fusion | bytes 33554432 | tf_op jit(solution)/shard_map/slice | solution.py:65
  431.2 10.8 %squeeze.4 = f32[1,64,2,128,128]{3,2,4,1,0:T(2,128)} reshape(f32[1,64,256,128]{2,3,0,1:T(8,128)} %get-tuple-element.29) | data formatting | bytes 16777216 | tf_op jit(solution)/shard_map/squeeze | solution.py:65
  442.1 10.8 %squeeze.5 = f32[1,64,2,128,128]{3,2,4,1,0:T(2,128)} reshape(f32[1,64,256,128]{2,3,0,1:T(8,128)} %get-tuple-element.30) | data formatting | bytes 16777216 | tf_op jit(solution)/shard_map/squeeze | solution.py:65
  452.8 35.4 %add_convert_fusion.1 = (bf16[1,64,2,128,128]{3,4,0,2,1:T(8,128)(2,1)S(1)}, bf16[1,64,2,128,128]{3,4,0,2,1:T(8,128)(2,1)}) fusion(f32[1,64,2,128,128]{3,2,4,1,0:T(2,128)} %squeeze.5, f32[1,64,2,128,128]{3,2,4,1,0:T(2,128)} %squeeze.4, f32[2,128,128]{1,2,0:T(8,128)S(1)} %convert_multiply_fusion, f32[64]{0:T(128)S(1)} %mul.534, f32[64]{0:T(128)S(1)} %div.46), kind=kLoop, calls=%fused_computation.24 | loop fusion | flops 23068672 | bytes 25297408 | tf_op jit(solution)/shard_map/convert.16
  488.2 4.6 convolution_bitcast_fusion
  492.8 3.8 add_convert_fusion
  496.6 4.6 fusion.14
  501.2 9.8 %copy.37 = bf16[64,2,32,2,4,128]{5,4,3,0,2,1:T(4,128)(2,1)} copy(bf16[64,2,32,2,4,128]{5,2,4,3,1,0:T(8,128)(2,1)S(1)} %fusion.14) | data formatting | bytes 16777216 | tf_op jit(solution)/shard_map/convert_element_type | solution.py:117
  511.1 14.3 %reshape_reshape.3 = bf16[4,16,2,8,4,1024]{5,1,0,4,3,2:T(8,128)(2,1)} reshape(bf16[64,2,32,2,4,128]{5,4,3,0,2,1:T(4,128)(2,1)} %copy.37) | data formatting | bytes 16777216 | tf_op jit(solution)/shard_map/reshape;reshape | solution.py:155
  525.4 8.7 copy.38
  534.1 188.9 %all_to_all.33 = bf16[4,16,2,8,4,1024]{5,1,0,4,2,3:T(8,128)(2,1)} all-to-all(bf16[4,16,2,8,4,1024]{5,1,0,4,2,3:T(8,128)(2,1)} %copy.38), channel_id=1, replica_groups=mesh['tm'=8,'sta'=4] {'tm'}, dimensions={3} | all-to-all | bytes 16777216 | tf_op jit(solution)/shard_map/all_to_all | solution.py:157
  723.0 8.7 copy.39
  731.7 8.5 copy.40
  740.2 100.8 %all_to_all.34 = bf16[4,16,16,1,4,1024]{5,1,2,0,3,4:T(8,128)(2,1)} all-to-all(bf16[4,16,16,1,4,1024]{5,1,2,0,3,4:T(8,128)(2,1)} %copy.40), channel_id=1, replica_groups=mesh['tm'=8,'sta'=4] {'sta'}, dimensions={4} | all-to-all | bytes 16777216 | tf_op jit(solution)/shard_map/all_to_all | solution.py:156
  841.0 12.8 %copy.41 = bf16[4,4,16,16,1,1,1024]{6,3,2,1,0,5,4:T(8,128)(2,1)} copy(bf16[4,4,16,16,1,1,1024]{6,2,3,0,1,5,4:T(8,128)(2,1)} %bitcast.96) | data formatting | bytes 16777216 | tf_op jit(solution)/shard_map/all_to_all | solution.py:156
  853.9 14.5 %reshape.488 = bf16[4,64,16,2,512]{4,3,2,1,0:T(2,128)(2,1)} reshape(bf16[4,4,16,16,1,1,1024]{6,3,2,1,0,5,4:T(8,128)(2,1)} %copy.41) | data formatting | bytes 16777216 | tf_op jit(solution)/shard_map/reshape | solution.py:163
  868.3 28.7 %copy.45 = bf16[4,64,16,2,512]{1,2,3,4,0:T(8,128)(2,1)} copy(bf16[4,64,16,2,512]{4,3,2,1,0:T(2,128)(2,1)} %reshape.488) | data formatting | bytes 16777216 | tf_op jit(solution)/shard_map/reshape | solution.py:163
  897.1 11.6 %slice_negate_fusion = (bf16[4,64,16,1,512]{1,2,3,4,0:T(8,128)(2,1)}, bf16[4,64,16,1,512]{1,2,3,4,0:T(8,128)(2,1)}) fusion(bf16[4,64,16,2,512]{1,2,3,4,0:T(8,128)(2,1)} %copy.45), kind=kLoop, calls=%fused_computation.11 | loop fusion | flops 2097152 | bytes 16777216 | tf_op jit(solution)/shard_map/neg | solution.py:122
  908.7 43.3 %bitcast_multiply_fusion = f32[4,512,64,128]{3,2,1,0:T(8,128)} fusion(bf16[4,64,16,2,512]{1,2,3,4,0:T(8,128)(2,1)} %copy.45, bf16[4,64,16,1,512]{1,2,3,4,0:T(8,128)(2,1)} %get-tuple-element.28, bf16[4,64,16,1,512]{1,2,3,4,0:T(8,128)(2,1)} %get-tuple-element.27), kind=kOutput, calls=%fused_computation.2 | convolution fusion | flops 1140850688 | bytes 83886080 | tf_op jit(solution)/shard_map/bifck,bjfck->bkij/dot_general | solution.py:124
  (212 shorter events, 187.8 us)
Async XLA Ops:
  17.6 51.4 %collective-permute-start = (bf16[2,64,8223]{2,0,1:T(2,128)(2,1)}, bf16[2,64,8223]{2,0,1:T(2,128)(2,1)S(1)}, u32[]{:S(2)}, u32[]{:S(2)}) collective-permute-start(bf16[2,64,8223]{2,0,1:T(2,128)(2,1)} %slice.65), channel_id=1, source_target_pairs={{4,0},{8,4},{12,8},{16,12},{20,16},{24,20},{28,24},{5,1},{9,5},{13... | collective-permute-start | bytes 6315272 | tf_op jit(solution)/shard_map/ppermute | solution.py:19
  19.3 7.0 copy-start.6
  19.4 7.1 copy-start.5
  19.4 7.2 copy-start.4
  19.4 9.3 copy-start.7
  389.6 2.0 copy-start
  452.8 35.4 %copy-start.1 = (bf16[1,128,2,128]{3,1,2,0:T(8,128)(2,1)S(1)}, bf16[1,128,2,128]{3,1,2,0:T(8,128)(2,1)}, u32[]{:S(2)}) copy-start(bf16[1,128,2,128]{3,1,2,0:T(8,128)(2,1)} %get-tuple-element.32) | copy-start | bytes 196612
  492.8 3.8 copy-start.2
  492.8 3.8 copy-start.3
where the time goes:
time: 966 us; the launch traced here: 952 us
  local copies, waits for them, and re-layouts  486 us (50%)
  blocking collectives  290 us (30%)
  matrix products  81 us (8%)
  other arithmetic  56.5 us (6%)
  waiting for transfers between devices  36.5 us (4%)
    gather x192, local copies, waits for them, and re-layouts  235 us
    all_to_all x1, blocking collectives, local(): lax.all_to_all(packed, 'tm', split_axis=3, concat_axis=2, tiled=True)  189 us
    all_to_all x1, blocking collectives, local(): lax.all_to_all(lax.all_to_all(packed, 'tm', split_axis=3, concat_axis=2,...  101 us
    unnamed x20, local copies, waits for them, and re-layouts  84.5 us
    dot_general x1, matrix products, correlate(): jnp.einsum('bifck,bjfck->bkij', spectra, partner, preferred_element_type=...  43.3 us
    reshape x2, local copies, waits for them, and re-layouts, local(): received.reshape(band_count, station_count * groups, slices * frames, 2,...  43.2 us
    another operation x5, other arithmetic  40.7 us
    ppermute x1, waiting for transfers between devices, shifted(): lax.ppermute(value, axis, [(source, source + steps) for source in range(f...  36.5 us
  transfers between devices with their start and end apart: 1, of which 1 were waited for; matrix products, arithmetic and copies ran while one was open for 1% of the time, Pallas kernels for 0%

commit v1 on v0

--- a/solution.py
+++ b/solution.py
@@ -11,6 +11,22 @@
 NFRAC = 64
 NPHASE = 1024
 MAXD = 8192
+
+
+def pairwise_exchange(x, axis, split, join):
+    ways, here = (lax.axis_size(axis), lax.axis_index(axis))
+    width = x.shape[split] // ways
+    shape = list(x.shape)
+    shape[split] = width
+    height = shape[join]
+    shape[join] = height * ways
+    full = jnp.zeros(shape, x.dtype)
+    for mask in range(ways):
+        part = lax.dynamic_slice_in_dim(x, (here ^ mask) * width, width, axis=split)
+        if mask:
+            part = lax.ppermute(part, axis, [(d, d ^ mask) for d in range(ways)])
+        full = lax.dynamic_update_slice_in_dim(full, part, (here ^ mask) * height, axis=join)
+    return full
 
 
 def shifted(value, axis, steps):
@@ -154,11 +170,7 @@
     spectra = transform(rotated, dft_tables(), block_width)
     packed = spectra.reshape(band_count, station_count, frames, slices, groups, 2 * block_width)
     received = lax.all_to_all(
-        lax.all_to_all(packed, "tm", split_axis=3, concat_axis=2, tiled=True),
-        "sta",
-        split_axis=4,
-        concat_axis=1,
-        tiled=True,
+        pairwise_exchange(packed, "tm", 3, 2), "sta", split_axis=4, concat_axis=1, tiled=True
     )
     gathered = received.reshape(band_count, station_count * groups, slices * frames, 2, block_width)
     return correlate(gathered)

time: 966 us -> 939 us (0.972)
  the two profiles are of different devices: /device:TPU:0 before, /device:TPU:8 now
where the time goes in v1:
time: 939 us; the launch traced here: 925 us
  local copies, waits for them, and re-layouts  482 us (51%)
  waiting for transfers between devices  195 us (21%)
  blocking collectives  96.9 us (10%)
  matrix products  81 us (9%)
  other arithmetic  56.9 us (6%)
  starting transfers between devices  13.4 us (1%)
    gather x192, local copies, waits for them, and re-layouts  235 us
    ppermute x7, waiting for transfers between devices, pairwise_exchange(): part = lax.ppermute(part, axis, [(d, d ^ mask) for d in range(ways)])  161 us
    all_to_all x1, blocking collectives, local(): lax.all_to_all(pairwise_exchange(packed, 'tm', 3, 2), 'sta', split_axis=4...  96.9 us
    unnamed x22, local copies, waits for them, and re-layouts  84.6 us
    reshape x2, local copies, waits for them, and re-layouts, local(): received.reshape(band_count, station_count * groups, slices * frames, 2,...  43.3 us
    dot_general x1, matrix products, correlate(): jnp.einsum('bifck,bjfck->bkij', spectra, partner, preferred_element_type=...  43.3 us
    another operation x5, other arithmetic  41.1 us
    ppermute x1, waiting for transfers between devices, shifted(): lax.ppermute(value, axis, [(source, source + steps) for source in range(f...  33.4 us
  transfers between devices with their start and end apart: 8, of which 6 were waited for; matrix products, arithmetic and copies ran while one was open for 3% of the time, Pallas kernels for 0%

profile of v1, /device:TPU:8, one launch (start us, length us, event | category | flops | bytes accessed | tf_op | source)
XLA Modules:
  0.0 925.5 jit_solution(11979893565106930996)
XLA Ops:
  0.0 14.6 %copy.34 = bf16[2,4,16,32768]{3,0,2,1:T(2,128)(2,1)S(1)} copy(bf16[2,4,16,32768]{3,2,1,0:T(8,128)(2,1)} %param.5) | data formatting | bytes 16777216 | tf_op args[0]
  17.6 3.6 collective-permute-start
  21.2 7.0 constant_dynamic-update-slice_fusion
  34.3 33.4 %collective-permute-done = bf16[2,64,8223]{2,0,1:T(2,128)(2,1)S(1)} collective-permute-done((bf16[2,64,8223]{2,0,1:T(2,128)(2,1)}, bf16[2,64,8223]{2,0,1:T(2,128)(2,1)S(1)}, u32[]{:S(2)}, u32[]{:S(2)}) %collective-permute-start) | collective-permute-done | bytes 2105120 | tf_op jit(solution)/shard_map/ppermute | solution.py:35
  67.7 60.9 %dynamic-update-slice.3 = bf16[2,64,41088]{2,0,1:T(2,128)(2,1)} dynamic-update-slice(bf16[2,64,41088]{2,0,1:T(2,128)(2,1)} %constant_dynamic-update-slice_fusion, bf16[2,64,8223]{2,0,1:T(2,128)(2,1)S(1)} %collective-permute-done, s32[]{} %constant.169, s32[]{} %constant.169, s32[]{} %constant.170) | dynamic-update-slice | bytes 4210180
  128.7 10.2 %dynamic-update-slice.4 = bf16[2,64,41088]{2,0,1:T(2,128)(2,1)} dynamic-update-slice(bf16[2,64,41088]{2,0,1:T(2,128)(2,1)} %dynamic-update-slice.3, bf16[2,64,97]{2,0,1:T(2,128)(2,1)S(1)} %broadcast_in_dim.28, s32[]{} %constant.169, s32[]{} %constant.169, s32[]{} %constant.171) | dynamic-update-slice | bytes 49668 | tf_op jit(solution)/shard_map/concatenate | solution.py:163
  138.8 234.7 %while.1 = (s32[]{:T(128)}, bf16[64,2,41088]{2,1,0:T(2,128)(2,1)}, s32[64,3]{0,1:T(4,128)S(1)}, bf16[64,2,32896]{2,1,0:T(2,128)(2,1)}, s32[]{:T(128)}) while((s32[]{:T(128)}, bf16[64,2,41088]{2,1,0:T(2,128)(2,1)}, s32[64,3]{0,1:T(4,128)S(1)}, bf16[64,2,32896]{2,1,0:T(2,128)(2,1)}, s32[]{:T(128)}) %tuple.39), condition=%wide.while_cond, body=%wide.while_body.sunk | while | flops 2 | bytes 264309 | solution.py:53
  150.5 3.0 dynamic-slice_dynamic-update-slice_fusion.2
  172.5 3.0 dynamic-slice_dynamic-update-slice_fusion.2
  179.8 3.0 dynamic-slice_dynamic-update-slice_fusion.2
  183.5 3.0 dynamic-slice_dynamic-update-slice_fusion.2
  223.8 3.0 dynamic-slice_dynamic-update-slice_fusion.2
  264.2 3.0 dynamic-slice_dynamic-update-slice_fusion.2
  297.1 3.0 dynamic-slice_dynamic-update-slice_fusion.2
  304.5 3.0 dynamic-slice_dynamic-update-slice_fusion.2
  326.5 3.0 dynamic-slice_dynamic-update-slice_fusion.2
  341.2 3.0 dynamic-slice_dynamic-update-slice_fusion.2
  359.5 3.0 dynamic-slice_dynamic-update-slice_fusion.2
  366.8 3.0 dynamic-slice_dynamic-update-slice_fusion.2
  370.5 3.0 dynamic-slice_dynamic-update-slice_fusion.2
  373.5 14.2 %reshape.521 = bf16[2,64,257,128]{3,2,0,1:T(8,128)(2,1)} reshape(bf16[2,64,32896]{2,0,1:T(2,128)(2,1)} %bitcast.93) | data formatting | bytes 16842752 | tf_op jit(solution)/shard_map/reshape | solution.py:62
  390.2 11.9 %fusion.6 = f32[64,128,2,256]{3,1,2,0:T(8,128)} fusion(bf16[2,64,257,128]{3,2,0,1:T(8,128)(2,1)} %reshape.521, bf16[64,256,128]{1,2,0:T(8,128)(2,1)S(1)} %bitcast.91), kind=kOutput, calls=%fused_computation.13 | convolution fusion | flops 1073741824 | bytes 27262976 | tf_op jit(solution)/shard_map/crnp,rpv->crnv/dot_general | solution.py:63
  402.1 16.7 %add_bitcast_fusion = f32[2,64,256,128]{2,3,0,1:T(8,128)} fusion(f32[64,128,2,256]{3,1,2,0:T(8,128)} %fusion.6, bf16[2,64,257,128]{3,2,0,1:T(8,128)(2,1)} %reshape.521, bf16[64,256,128]{1,2,0:T(8,128)(2,1)} %bitcast.92), kind=kOutput, calls=%fused_computation.9 | convolution fusion | flops 1077936128 | bytes 44040192 | tf_op jit(solution)/shard_map/crnp,rpv->crnv/dot_general | solution.py:66
  418.8 11.1 %fusion.78 = (f32[1,64,256,128]{2,3,0,1:T(8,128)}, f32[1,64,256,128]{2,3,0,1:T(8,128)}) fusion(f32[2,64,256,128]{2,3,0,1:T(8,128)} %add_bitcast_fusion), kind=kLoop, calls=%fused_computation.146 | loop fusion | bytes 33554432 | tf_op jit(solution)/shard_map/slice | solution.py:81
  429.9 10.9 %squeeze.4 = f32[1,64,2,128,128]{3,2,4,1,0:T(2,128)} reshape(f32[1,64,256,128]{2,3,0,1:T(8,128)} %get-tuple-element.29) | data formatting | bytes 16777216 | tf_op jit(solution)/shard_map/squeeze | solution.py:81
  440.8 10.8 %squeeze.5 = f32[1,64,2,128,128]{3,2,4,1,0:T(2,128)} reshape(f32[1,64,256,128]{2,3,0,1:T(8,128)} %get-tuple-element.30) | data formatting | bytes 16777216 | tf_op jit(solution)/shard_map/squeeze | solution.py:81
  451.5 35.7 %add_convert_fusion.1 = (bf16[1,64,2,128,128]{3,4,0,2,1:T(8,128)(2,1)S(1)}, bf16[1,64,2,128,128]{3,4,0,2,1:T(8,128)(2,1)}) fusion(f32[1,64,2,128,128]{3,2,4,1,0:T(2,128)} %squeeze.5, f32[1,64,2,128,128]{3,2,4,1,0:T(2,128)} %squeeze.4, f32[2,128,128]{1,2,0:T(8,128)S(1)} %convert_multiply_fusion, f32[64]{0:T(128)S(1)} %mul.558, f32[64]{0:T(128)S(1)} %div.46), kind=kLoop, calls=%fused_computation.24 | loop fusion | flops 23068672 | bytes 25297408 | tf_op jit(solution)/shard_map/convert.16
  487.3 4.6 convolution_bitcast_fusion
  491.9 3.8 add_convert_fusion
  495.7 4.6 fusion.14
  500.3 9.8 %copy.43 = bf16[64,2,32,2,4,128]{5,4,3,0,2,1:T(4,128)(2,1)} copy(bf16[64,2,32,2,4,128]{5,2,4,3,1,0:T(8,128)(2,1)S(1)} %fusion.14) | data formatting | bytes 16777216 | tf_op jit(solution)/shard_map/convert_element_type | solution.py:133
  510.1 14.5 %reshape_reshape.3 = bf16[4,16,2,8,4,1024]{5,1,0,4,3,2:T(8,128)(2,1)} reshape(bf16[64,2,32,2,4,128]{5,4,3,0,2,1:T(4,128)(2,1)} %copy.43) | data formatting | bytes 16777216 | tf_op jit(solution)/shard_map/reshape;reshape | solution.py:171
  524.6 6.4 constant_dynamic-slice_fusion.1
  534.8 3.0 collective-permute-start.7
  542.0 58.9 %collective-permute-done.1 = bf16[4,16,2,1,4,1024]{5,1,0,4,3,2:T(8,128)(2,1)} collective-permute-done((bf16[4,16,2,1,4,1024]{5,1,0,4,3,2:T(8,128)(2,1)}, bf16[4,16,2,1,4,1024]{5,1,0,4,3,2:T(8,128)(2,1)}, u32[]{:S(2)}, u32[]{:S(2)}) %collective-permute-start.1) | collective-permute-done | bytes 1048608 | tf_op jit(solution)/shard_map/ppermute | solution.py:27
  600.9 3.0 copy_dynamic-update-slice_fusion.6
  605.6 3.0 copy_dynamic-update-slice_fusion.5
  608.6 14.3 %collective-permute-done.3 = bf16[4,16,2,1,4,1024]{5,1,0,4,3,2:T(8,128)(2,1)} collective-permute-done((bf16[4,16,2,1,4,1024]{5,1,0,4,3,2:T(8,128)(2,1)}, bf16[4,16,2,1,4,1024]{5,1,0,4,3,2:T(8,128)(2,1)}, u32[]{:S(2)}, u32[]{:S(2)}) %collective-permute-start.3) | collective-permute-done | bytes 1048608 | tf_op jit(solution)/shard_map/ppermute | solution.py:27
  622.9 3.0 copy_dynamic-update-slice_fusion.4
  625.9 45.9 %collective-permute-done.4 = bf16[4,16,2,1,4,1024]{5,1,0,4,3,2:T(8,128)(2,1)S(1)} collective-permute-done((bf16[4,16,2,1,4,1024]{5,1,0,4,3,2:T(8,128)(2,1)}, bf16[4,16,2,1,4,1024]{5,1,0,4,3,2:T(8,128)(2,1)S(1)}, u32[]{:S(2)}, u32[]{:S(2)}) %collective-permute-start.4) | collective-permute-done | bytes 1048608 | tf_op jit(solution)/shard_map/ppermute | solution.py:27
  673.7 20.6 %collective-permute-done.5 = bf16[4,16,2,1,4,1024]{5,1,0,4,3,2:T(8,128)(2,1)S(1)} collective-permute-done((bf16[4,16,2,1,4,1024]{5,1,0,4,3,2:T(8,128)(2,1)S(1)}, bf16[4,16,2,1,4,1024]{5,1,0,4,3,2:T(8,128)(2,1)S(1)}, u32[]{:S(2)}, u32[]{:S(2)}) %collective-permute-start.5) | collective-permute-done | bytes 1048608 | tf_op jit(solution)/shard_map/ppermute | solution.py:27
  696.3 21.6 %collective-permute-done.6 = bf16[4,16,2,1,4,1024]{5,1,0,4,3,2:T(8,128)(2,1)S(1)} collective-permute-done((bf16[4,16,2,1,4,1024]{5,1,0,4,3,2:T(8,128)(2,1)S(1)}, bf16[4,16,2,1,4,1024]{5,1,0,4,3,2:T(8,128)(2,1)S(1)}, u32[]{:S(2)}, u32[]{:S(2)}) %collective-permute-start.6) | collective-permute-done | bytes 1048608 | tf_op jit(solution)/shard_map/ppermute | solution.py:27
  721.5 96.9 %all_to_all.15 = bf16[4,16,16,1,4,1024]{5,2,1,0,3,4:T(8,128)(2,1)} all-to-all(bf16[4,16,16,1,4,1024]{5,2,1,0,3,4:T(8,128)(2,1)S(1)} %copy_dynamic-update-slice_fusion), channel_id=1, replica_groups=mesh['tm'=8,'sta'=4] {'sta'}, dimensions={4} | all-to-all | bytes 16777216 | tf_op jit(solution)/shard_map/all_to_all | solution.py:172
  818.4 8.7 copy.52
  827.1 14.5 %reshape.488 = bf16[4,64,16,2,512]{4,3,2,1,0:T(2,128)(2,1)} reshape(bf16[4,4,16,16,1,1,1024]{6,3,2,1,0,5,4:T(8,128)(2,1)} %copy.52) | data formatting | bytes 16777216 | tf_op jit(solution)/shard_map/reshape | solution.py:175
  841.6 28.8 %copy.56 = bf16[4,64,16,2,512]{1,2,3,4,0:T(8,128)(2,1)} copy(bf16[4,64,16,2,512]{4,3,2,1,0:T(2,128)(2,1)} %reshape.488) | data formatting | bytes 16777216 | tf_op jit(solution)/shard_map/reshape | solution.py:175
  870.3 11.6 %slice_negate_fusion = (bf16[4,64,16,1,512]{1,2,3,4,0:T(8,128)(2,1)}, bf16[4,64,16,1,512]{1,2,3,4,0:T(8,128)(2,1)}) fusion(bf16[4,64,16,2,512]{1,2,3,4,0:T(8,128)(2,1)} %copy.56), kind=kLoop, calls=%fused_computation.11 | loop fusion | flops 2097152 | bytes 16777216 | tf_op jit(solution)/shard_map/neg | solution.py:138
  882.0 43.3 %bitcast_multiply_fusion = f32[4,512,64,128]{3,2,1,0:T(8,128)} fusion(bf16[4,64,16,2,512]{1,2,3,4,0:T(8,128)(2,1)} %copy.56, bf16[4,64,16,1,512]{1,2,3,4,0:T(8,128)(2,1)} %get-tuple-element.28, bf16[4,64,16,1,512]{1,2,3,4,0:T(8,128)(2,1)} %get-tuple-element.27), kind=kOutput, calls=%fused_computation.2 | convolution fusion | flops 1140850688 | bytes 83886080 | tf_op jit(solution)/shard_map/bifck,bjfck->bkij/dot_general | solution.py:140
  (234 shorter events, 223.9 us)
Async XLA Ops:
  17.6 50.2 %collective-permute-start = (bf16[2,64,8223]{2,0,1:T(2,128)(2,1)}, bf16[2,64,8223]{2,0,1:T(2,128)(2,1)S(1)}, u32[]{:S(2)}, u32[]{:S(2)}) collective-permute-start(bf16[2,64,8223]{2,0,1:T(2,128)(2,1)} %slice.65), channel_id=1, source_target_pairs={{4,0},{8,4},{12,8},{16,12},{20,16},{24,20},{28,24},{5,1},{9,5},{13... | collective-permute-start | bytes 6315272 | tf_op jit(solution)/shard_map/ppermute | solution.py:35
  21.2 7.0 copy-start.7
  21.2 7.1 copy-start.6
  21.2 7.2 copy-start.5
  21.2 9.4 %copy-start.8 = (s32[16,1]{0,1:T(1,128)S(1)}, s32[16,1]{0,1:T(1,128)}, u32[]{:S(2)}) copy-start(s32[16,1]{0,1:T(1,128)} %param.7) | copy-start | bytes 196
  388.2 2.0 copy-start
  451.5 35.8 %copy-start.2 = (bf16[1,128,2,128]{3,1,2,0:T(8,128)(2,1)S(1)}, bf16[1,128,2,128]{3,1,2,0:T(8,128)(2,1)}, u32[]{:S(2)}) copy-start(bf16[1,128,2,128]{3,1,2,0:T(8,128)(2,1)} %get-tuple-element.40) | copy-start | bytes 196612
  491.8 3.8 copy-start.3
  491.9 3.8 copy-start.4
  531.0 69.9 %collective-permute-start.1 = (bf16[4,16,2,1,4,1024]{5,1,0,4,3,2:T(8,128)(2,1)}, bf16[4,16,2,1,4,1024]{5,1,0,4,3,2:T(8,128)(2,1)}, u32[]{:S(2)}, u32[]{:S(2)}) collective-permute-start(bf16[4,16,2,1,4,1024]{5,1,0,4,3,2:T(8,128)(2,1)} %get-tuple-element.37), channel_id=1, source_target_pairs={{0,4},{4,0},{8,12},{12,8},{16,20},{20,16},{24,28},{28,24},{1,5},{5... | collective-permute-start | bytes 3145736 | tf_op jit(solution)/shard_map/ppermute | solution.py:27
  533.4 70.6 %collective-permute-start.2 = (bf16[4,16,2,1,4,1024]{5,1,0,4,3,2:T(8,128)(2,1)}, bf16[4,16,2,1,4,1024]{5,1,0,4,3,2:T(8,128)(2,1)}, u32[]{:S(2)}, u32[]{:S(2)}) collective-permute-start(bf16[4,16,2,1,4,1024]{5,1,0,4,3,2:T(8,128)(2,1)} %get-tuple-element.36), channel_id=1, source_target_pairs={{0,8},{4,12},{8,0},{12,4},{16,24},{20,28},{24,16},{28,20},{1,9},{5... | collective-permute-start | bytes 3145736 | tf_op jit(solution)/shard_map/ppermute | solution.py:27
  533.8 89.1 %collective-permute-start.3 = (bf16[4,16,2,1,4,1024]{5,1,0,4,3,2:T(8,128)(2,1)}, bf16[4,16,2,1,4,1024]{5,1,0,4,3,2:T(8,128)(2,1)}, u32[]{:S(2)}, u32[]{:S(2)}) collective-permute-start(bf16[4,16,2,1,4,1024]{5,1,0,4,3,2:T(8,128)(2,1)} %get-tuple-element.35), channel_id=1, source_target_pairs={{0,12},{4,8},{8,4},{12,0},{16,28},{20,24},{24,20},{28,16},{1,13},{... | collective-permute-start | bytes 3145736 | tf_op jit(solution)/shard_map/ppermute | solution.py:27
  534.8 66.1 %copy-start.1 = (bf16[4,16,2,1,4,1024]{5,1,0,4,3,2:T(8,128)(2,1)S(1)}, bf16[4,16,2,1,4,1024]{5,1,0,4,3,2:T(8,128)(2,1)}, u32[]{:S(2)}) copy-start(bf16[4,16,2,1,4,1024]{5,1,0,4,3,2:T(8,128)(2,1)} %get-tuple-element.33) | copy-start | bytes 3145732
  534.8 184.8 %collective-permute-start.7 = (bf16[4,16,2,1,4,1024]{5,1,0,4,3,2:T(8,128)(2,1)S(1)}, bf16[4,16,2,1,4,1024]{5,1,0,4,3,2:T(8,128)(2,1)S(1)}, u32[]{:S(2)}, u32[]{:S(2)}) collective-permute-start(bf16[4,16,2,1,4,1024]{5,1,0,4,3,2:T(8,128)(2,1)S(1)} %get-tuple-element.31), channel_id=1, source_target_pairs={{0,28},{4,24},{8,20},{12,16},{16,12},{20,8},{24,4},{28,0},{1,29},{... | collective-permute-start | bytes 3145736 | tf_op jit(solution)/shard_map/ppermute | solution.py:27
  537.9 134.0 %collective-permute-start.4 = (bf16[4,16,2,1,4,1024]{5,1,0,4,3,2:T(8,128)(2,1)}, bf16[4,16,2,1,4,1024]{5,1,0,4,3,2:T(8,128)(2,1)S(1)}, u32[]{:S(2)}, u32[]{:S(2)}) collective-permute-start(bf16[4,16,2,1,4,1024]{5,1,0,4,3,2:T(8,128)(2,1)} %get-tuple-element.34), channel_id=1, source_target_pairs={{0,16},{4,20},{8,24},{12,28},{16,0},{20,4},{24,8},{28,12},{1,17},{... | collective-permute-start | bytes 3145736 | tf_op jit(solution)/shard_map/ppermute | solution.py:27
  600.9 93.3 %collective-permute-start.5 = (bf16[4,16,2,1,4,1024]{5,1,0,4,3,2:T(8,128)(2,1)S(1)}, bf16[4,16,2,1,4,1024]{5,1,0,4,3,2:T(8,128)(2,1)S(1)}, u32[]{:S(2)}, u32[]{:S(2)}) collective-permute-start(bf16[4,16,2,1,4,1024]{5,1,0,4,3,2:T(8,128)(2,1)S(1)} %copy-done.1), channel_id=1, source_target_pairs={{0,20},{4,16},{8,28},{12,24},{16,4},{20,0},{24,12},{28,8},{1,21},{... | collective-permute-start | bytes 3145736 | tf_op jit(solution)/shard_map/ppermute | solution.py:27
  604.0 113.9 %collective-permute-start.6 = (bf16[4,16,2,1,4,1024]{5,1,0,4,3,2:T(8,128)(2,1)S(1)}, bf16[4,16,2,1,4,1024]{5,1,0,4,3,2:T(8,128)(2,1)S(1)}, u32[]{:S(2)}, u32[]{:S(2)}) collective-permute-start(bf16[4,16,2,1,4,1024]{5,1,0,4,3,2:T(8,128)(2,1)S(1)} %get-tuple-element.32), channel_id=1, source_target_pairs={{0,24},{4,28},{8,16},{12,20},{16,8},{20,12},{24,0},{28,4},{1,25},{... | collective-permute-start | bytes 3145736 | tf_op jit(solution)/shard_map/ppermute | solution.py:27
